TPU v7x, 32 devices: a whole 2x2x4 slice. The times are simulated.
32 devices in a mesh: col: 16 (over z, y, x), row: 2 (over core).
Axes of the slice: x: 2, y: 2, z: 4, core: 2. Of those that a mesh axis runs over, the one named last changes fastest.
Arguments:
- k_blocks: bfloat16 [2, 16, 4, 256, 256], P('row', 'col'), may hold values from -0.1875 to 0.1875
- slot_row: int32 [2, 16, 4], P('row', 'col'), may hold values from 0 to 3
- slot_col: int32 [2, 16, 4], P('row', 'col'), may hold values from 0 to 3
- live_count: int32 [2, 16], P('row', 'col'), may hold values from 1 to 4, as said below
- cost: float32 [16384], P('col'), may hold values from -6 to 6
- upper: float32 [16384], P('col'), may hold values from 0.5 to 2
- tau: float32 [16384], P('col'), may hold values from 0.2 to 0.8
- sigma: float32 [2, 1024], P('row', 'col'), may hold values from 0.2 to 0.8
- demand: float32 [2, 1024, 128], P('row', 'col'), may hold values from -6 to 6
- primal_start: float32 [16384, 128], P('col'), may hold values from 0 to 1
- dual_start: float32 [2, 1024, 128], P('row', 'col'), may hold values from 0 to 1
Outputs:
- primal: float32 [16384, 128], P('col')
- dual: float32 [2, 1024, 128], P('row', 'col')
Inputs may be any that keep to these rules, and one draw needn't show every extreme that they name: `live_count`: only slots below a device's count belong to K; the blocks in later slots are ignored. Some device has all 4 slots in use.
All inputs are finite; a program needn't handle non-finite values.
Results may differ from a plain program's by a relative error of at most 0.0023.
Values may be sent and summed in bfloat16 or wider, within the bound.
A program may use at most 64 MiB of HBM per device.

v0:
```python
import jax
import jax.numpy as jnp
from jax import lax
from jax.sharding import PartitionSpec as P

ITERS = 2


def transpose_terms(blocks, row_hot, col_hot, everyone):
    chosen = jnp.einsum(
        "kg,gis->kis", row_hot.astype(jnp.bfloat16), everyone, preferred_element_type=jnp.float32
    ).astype(jnp.bfloat16)
    terms = jnp.einsum("kij,kis->kjs", blocks, chosen, preferred_element_type=jnp.float32)
    return jnp.einsum(
        "kc,kjs->cjs", col_hot.astype(jnp.float32), terms, precision=lax.Precision.HIGHEST
    )


def forward_terms(blocks, row_hot, col_hot, extrapolated):
    chosen = jnp.einsum(
        "kc,cjs->kjs",
        col_hot.astype(jnp.bfloat16),
        extrapolated,
        preferred_element_type=jnp.float32,
    ).astype(jnp.bfloat16)
    terms = jnp.einsum("kij,kjs->kis", blocks, chosen, preferred_element_type=jnp.float32)
    return jnp.einsum(
        "kg,kis->gis", row_hot.astype(jnp.float32), terms, precision=lax.Precision.HIGHEST
    )


def on_device(
    k_blocks,
    slot_row,
    slot_col,
    live_count,
    cost,
    upper,
    tau,
    sigma,
    demand,
    primal_start,
    dual_start,
):
    blocks = k_blocks[0, 0]
    rows_of = slot_row[0, 0]
    cols_of = slot_col[0, 0]
    count = live_count[0, 0]
    slots = blocks.shape[0]
    width = blocks.shape[1]
    col_count = lax.axis_size("col")
    groups = col_count // 4
    scenarios = primal_start.shape[1]
    col_blocks = primal_start.shape[0] // width
    live = jnp.arange(slots) < count
    row_hot = (rows_of[:, None] == jnp.arange(groups)[None, :]) & live[:, None]
    col_hot = (cols_of[:, None] == jnp.arange(col_blocks)[None, :]) & live[:, None]
    primal = primal_start
    dual = dual_start[0]
    rates = sigma[0][:, None]
    needed = demand[0]
    for step in range(ITERS):
        everyone = lax.all_gather(dual.astype(jnp.bfloat16), "col", axis=0, tiled=True).reshape(
            groups, width, scenarios
        )
        per_col = transpose_terms(blocks, row_hot, col_hot, everyone)
        flat = per_col.reshape(col_blocks * width, scenarios)
        back = lax.psum(flat, "row")
        new_primal = jnp.minimum(
            jnp.maximum(primal - tau[:, None] * (cost[:, None] - back), 0.0), upper[:, None]
        )
        extrapolated = (
            (2.0 * new_primal - primal).astype(jnp.bfloat16).reshape(col_blocks, width, scenarios)
        )
        per_row = forward_terms(blocks, row_hot, col_hot, extrapolated)
        outgoing = per_row.reshape(col_count, -1, scenarios)
        incoming = lax.all_to_all(outgoing, "col", split_axis=0, concat_axis=0, tiled=True)
        forward = jnp.sum(incoming, axis=0)
        dual = jnp.maximum(dual + rates * (needed - forward), 0.0)
        primal = new_primal
    return (primal, dual[None])


def solution(mesh):
    in_specs = (
        P("row", "col", None, None, None),
        P("row", "col", None),
        P("row", "col", None),
        P("row", "col"),
        P("col"),
        P("col"),
        P("col"),
        P("row", "col"),
        P("row", "col", None),
        P("col", None),
        P("row", "col", None),
    )
    out_specs = (P("col", None), P("row", "col", None))
    return jax.shard_map(
        on_device, mesh=mesh, in_specs=in_specs, out_specs=out_specs, check_vma=False
    )
```

profile of v0, /device:TPU:0, one launch (start us, length us, event | category | flops | bytes accessed | tf_op | source)
XLA Modules:
  0.0 186.3 jit_solution(3237687826428789127)
XLA Ops:
  7.2 0.0 copy-start
  7.2 0.0 all-reduce.3.cloned.1.call-start
  7.9 0.8 bitcast_convert_fusion
  8.7 43.8 %all_gather.6 = bf16[1024,128]{1,0:T(8,128)(2,1)S(1)} all-gather(bf16[64,128]{1,0:T(8,128)(2,1)S(1)} %bitcast_convert_fusion), channel_id=1, replica_groups=mesh['col'=16,'row'=2] {'col'}, dimensions={0}, use_global_device_ids=true | all-gather | bytes 278528 | tf_op jit(solution)/shard_map/all_gather | solution.py:63
  52.5 0.0 copy-start.9
  52.5 0.0 copy-start.10
  52.5 0.7 copy-done.9
  53.1 0.0 copy-done.10
  53.1 0.4 fusion.22
  53.5 0.0 copy-done
  53.5 0.3 fusion.14
  53.8 0.2 copy.19
  54.0 0.6 fusion.6
  54.6 0.0 copy-start.6
  54.6 0.0 copy-start.7
  54.6 0.8 copy.13
  55.5 0.0 copy-start.1
  55.5 0.0 copy-start.5
  55.5 0.0 all-reduce.3.cloned.1.call-update
  55.5 0.0 all-reduce.5.cloned.1.call-start
  55.6 14.7 %all-reduce.3.cloned.1.call-done = f32[1024,128]{1,0:T(8,128)} async-done(((f32[1024,128]{1,0:T(8,128)}), f32[1024,128]{1,0:T(8,128)}) %all-reduce.3.cloned.1.call-update) | async-done | bytes 524304 | tf_op jit(solution)/shard_map/psum | solution.py:68
  70.3 0.0 copy-done.6
  70.3 0.0 copy-done.7
  70.3 0.0 copy-done.1
  70.3 0.0 copy-done.5
  70.3 1.5 subtract_convert_fusion.1
  71.8 0.4 fusion.20
  72.2 0.3 fusion.12
  72.5 0.2 copy.22
  72.7 0.6 fusion.4
  73.4 22.1 %all_to_all.10 = f32[16,64,128]{2,1,0:T(8,128)S(1)} all-to-all(f32[16,64,128]{2,1,0:T(8,128)S(1)} %bitcast.79), channel_id=1, replica_groups=mesh['col'=16,'row'=2] {'col'}, dimensions={0} | all-to-all | bytes 1048576 | tf_op jit(solution)/shard_map/all_to_all | solution.py:77
  95.4 0.0 copy-start.3
  95.4 0.0 copy-start.4
  95.5 0.0 copy-start.8
  95.5 0.7 copy-done.3
  96.2 0.0 copy-done.4
  96.2 0.0 copy-done.8
  96.2 0.1 fusion.33
  96.3 39.5 %all_gather.7 = bf16[1024,128]{1,0:T(8,128)(2,1)S(1)} all-gather(bf16[64,128]{1,0:T(8,128)(2,1)S(1)} %fusion.33), channel_id=1, replica_groups=mesh['col'=16,'row'=2] {'col'}, dimensions={0}, use_global_device_ids=true | all-gather | bytes 278528 | tf_op jit(solution)/shard_map/all_gather | solution.py:63
  135.7 0.4 fusion.18
  136.1 0.3 fusion.10
  136.4 0.2 copy.25
  136.6 0.6 fusion.2
  137.2 0.8 copy.15
  138.0 0.0 copy-start.2
  138.0 0.0 all-reduce.5.cloned.1.call-update
  138.1 14.8 %all-reduce.5.cloned.1.call-done = f32[1024,128]{1,0:T(8,128)} async-done(((f32[1024,128]{1,0:T(8,128)}), f32[1024,128]{1,0:T(8,128)}) %all-reduce.5.cloned.1.call-update) | async-done | bytes 524304 | tf_op jit(solution)/shard_map/psum | solution.py:68
  152.8 0.0 copy-done.2
  152.8 2.3 %subtract_convert_fusion = (bf16[1024,128]{1,0:T(8,128)(2,1)S(1)}, f32[1024,128]{1,0:T(8,128)}) fusion(f32[1024]{0:T(1024)S(1)} %copy-done.5, f32[1024,128]{1,0:T(8,128)S(1)} %copy-done.1, f32[1024,128]{1,0:T(8,128)S(1)} %copy-done.2, f32[1024]{0:T(1024)S(1)} %copy-done.6, f32[1024]{0:T(1024)S(1)} %copy-done.7, f32[1024,128]{1,0:T(8,128)} %all-reduce.5.cloned.1.call-done), kind=kLoop, calls=%fused_computation.20 | loop fusion | flops 1703936 | bytes 2371584 | tf_op jit(solution)/shard_map/convert_element_type | solution.py:73
  155.1 0.4 fusion.16
  155.5 0.3 fusion.8
  155.8 0.2 copy.28
  156.1 0.6 fusion
  156.7 22.1 %all_to_all.11 = f32[16,64,128]{2,1,0:T(8,128)S(1)} all-to-all(f32[16,64,128]{2,1,0:T(8,128)S(1)} %bitcast.80), channel_id=1, replica_groups=mesh['col'=16,'row'=2] {'col'}, dimensions={0} | all-to-all | bytes 1048576 | tf_op jit(solution)/shard_map/all_to_all | solution.py:77
  178.8 0.7 fusion.26
  (6 shorter events, 0.2 us)
Async XLA Ops:
  7.2 46.3 %copy-start = (bf16[1,1,4,256,256]{4,3,2,1,0:T(8,128)(2,1)S(1)}, bf16[1,1,4,256,256]{4,3,2,1,0:T(8,128)(2,1)}, u32[]{:S(2)}) copy-start(bf16[1,1,4,256,256]{4,3,2,1,0:T(8,128)(2,1)} %param.11) | copy-start | bytes 1572868
  7.2 63.1 %all-reduce.3.cloned.1.call-start = ((), (), s32[]{:S(2)}) async-start(), calls=%async_computation.2 | async-start | bytes 1048576 | tf_op jit(solution)/shard_map/psum | solution.py:68
  52.5 0.7 copy-start.9
  52.5 0.7 copy-start.10
  54.6 15.6 %copy-start.6 = (f32[1024]{0:T(1024)S(1)}, f32[1024]{0:T(1024)}, u32[]{:S(2)}) copy-start(f32[1024]{0:T(1024)} %param.15) | copy-start | bytes 12292
  54.6 15.6 %copy-start.7 = (f32[1024]{0:T(1024)S(1)}, f32[1024]{0:T(1024)}, u32[]{:S(2)}) copy-start(f32[1024]{0:T(1024)} %param.17) | copy-start | bytes 12292
  55.5 14.8 %copy-start.1 = (f32[1024,128]{1,0:T(8,128)S(1)}, f32[1024,128]{1,0:T(8,128)}, u32[]{:S(2)}) copy-start(f32[1024,128]{1,0:T(8,128)} %param.20) | copy-start | bytes 1572868
  55.5 14.8 %copy-start.5 = (f32[1024]{0:T(1024)S(1)}, f32[1024]{0:T(1024)}, u32[]{:S(2)}) copy-start(f32[1024]{0:T(1024)} %param.16) | copy-start | bytes 12292
  55.5 97.3 %all-reduce.5.cloned.1.call-start = ((), (), s32[]{:S(2)}) async-start(), calls=%async_computation.3 | async-start | bytes 1048576 | tf_op jit(solution)/shard_map/psum | solution.py:68
  95.4 0.8 copy-start.3
  95.4 0.8 copy-start.4
  95.5 0.7 copy-start.8
  138.0 14.8 %copy-start.2 = (f32[1024,128]{1,0:T(8,128)S(1)}, f32[1024,128]{1,0:T(8,128)}, u32[]{:S(2)}) copy-start(f32[1024,128]{1,0:T(8,128)} %all-reduce.3.cloned.1.call-done) | copy-start | bytes 1572868
Sparse Core Ops, SparseCore 0:
  55.6 14.5 all-reduce.2
  138.2 14.5 all-reduce.4
where the time goes:
time: 187 us; the launch traced here: 186 us
  blocking collectives  127 us (68%)
  waiting for transfers between devices  29.5 us (16%)
  between operations  14.9 us (8%)
  other arithmetic  5.45 us (3%)
  matrix products  4.98 us (3%)
  local copies, waits for them, and re-layouts  4.08 us (2%)
    all_gather x2, blocking collectives, on_device(): lax.all_gather(dual.astype(jnp.bfloat16), 'col', axis=0, tiled=True)  83.2 us
    all_to_all x2, blocking collectives, on_device(): lax.all_to_all(outgoing, 'col', split_axis=0, concat_axis=0, tiled=True)  44.1 us
    psum x2, waiting for transfers between devices, on_device(): back = lax.psum(flat, 'row')  29.5 us
    convert_element_type x2, other arithmetic, on_device(): (2.0 * new_primal - primal).astype(jnp.bfloat16)  3.83 us
  transfers between devices with their start and end apart: 2, of which 2 were waited for; matrix products, arithmetic and copies ran while one was open for 0% of the time, Pallas kernels for 0%

commit v1 on v0

--- a/solution.py
+++ b/solution.py
@@ -65,7 +65,8 @@
         )
         per_col = transpose_terms(blocks, row_hot, col_hot, everyone)
         flat = per_col.reshape(col_blocks * width, scenarios)
-        back = lax.psum(flat, "row")
+        terms_2 = lax.all_gather(flat, "row")
+        back = jnp.sum(terms_2, axis=0)
         new_primal = jnp.minimum(
             jnp.maximum(primal - tau[:, None] * (cost[:, None] - back), 0.0), upper[:, None]
         )

time: 187 us -> 168 us (0.90)
  waiting for transfers between devices: 29.5 us -> 10.1 us
    psum x2 -> x0, waiting for transfers between devices: 29.5 us -> none  [on_device(): back = lax.psum(flat, 'row')]
    all_gather x0 -> x2, waiting for transfers between devices: none -> 10 us  [on_device(): terms_2 = lax.all_gather(flat, 'row')]
    reduce_sum x0 -> x2, other arithmetic: none -> 2.68 us  [on_device(): back = jnp.sum(terms_2, axis=0)]
    convert_element_type x2, other arithmetic: 3.83 us -> 1.75 us  [on_device(): (2.0 * new_primal - primal).astype(jnp.bfloat16)]
where the time goes in v1:
time: 168 us
  blocking collectives  127 us (76%)
  between operations  15 us (9%)
  waiting for transfers between devices  10.1 us (6%)
  other arithmetic  6.06 us (4%)
  matrix products  4.98 us (3%)
  local copies, waits for them, and re-layouts  4.08 us (2%)
    all_gather x2, blocking collectives, on_device(): lax.all_gather(dual.astype(jnp.bfloat16), 'col', axis=0, tiled=True)  83.2 us
    all_to_all x2, blocking collectives, on_device(): lax.all_to_all(outgoing, 'col', split_axis=0, concat_axis=0, tiled=True)  44.1 us
    all_gather x2, waiting for transfers between devices, on_device(): terms_2 = lax.all_gather(flat, 'row')  10 us
  transfers between devices with their start and end apart: 2, of which 2 were waited for; matrix products, arithmetic and copies ran while one was open for 0% of the time, Pallas kernels for 0%

profile of v1, /device:TPU:0, one launch (start us, length us, event | category | flops | bytes accessed | tf_op | source)
XLA Modules:
  0.0 167.5 jit_solution(7236334171785039100)
XLA Ops:
  7.2 0.0 copy-start
  7.2 0.0 all-gather.3.cloned.1.call-start
  7.9 0.8 bitcast_convert_fusion
  8.7 43.8 %all_gather.12 = bf16[1024,128]{1,0:T(8,128)(2,1)S(1)} all-gather(bf16[64,128]{1,0:T(8,128)(2,1)S(1)} %bitcast_convert_fusion), channel_id=1, replica_groups=mesh['col'=16,'row'=2] {'col'}, dimensions={0}, use_global_device_ids=true | all-gather | bytes 278528 | tf_op jit(solution)/shard_map/all_gather | solution.py:63
  52.5 0.0 copy-start.8
  52.5 0.0 copy-start.9
  52.5 0.7 copy-done.8
  53.1 0.0 copy-done.9
  53.1 0.4 convolution_convert_fusion.3
  53.5 0.0 copy-done
  53.5 0.3 convolution_bitcast_fusion.3
  53.8 0.2 copy.38
  54.0 0.6 fusion.26
  54.6 0.8 copy.39
  55.4 0.0 all-gather.3.cloned.1.call-update
  55.5 0.0 copy-start.1
  55.5 0.0 copy-start.4
  55.5 0.0 copy-start.5
  55.5 0.0 copy-start.6
  55.5 0.0 all-gather.5.cloned.1.call-start
  55.6 5.0 %all-gather.3.cloned.1.call-done = f32[2,1024,128]{2,1,0:T(8,128)} async-done(((f32[1,1024,128]{2,1,0:T(8,128)}), f32[2,1024,128]{2,1,0:T(8,128)}) %all-gather.3.cloned.1.call-update) | async-done | bytes 1048592 | tf_op jit(solution)/shard_map/all_gather | solution.py:68
  60.5 1.3 reduce_sum.40
  61.9 0.0 copy-done.1
  61.9 0.0 copy-done.4
  61.9 0.0 copy-done.5
  61.9 0.0 copy-done.6
  61.9 0.5 subtract_convert_fusion.1
  62.4 0.4 convolution_convert_fusion.2
  62.8 0.3 convolution_bitcast_fusion.2
  63.1 0.2 copy.43
  63.3 0.6 fusion.27
  64.0 22.1 %all_to_all.10 = f32[16,64,128]{2,1,0:T(8,128)S(1)} all-to-all(f32[16,64,128]{2,1,0:T(8,128)S(1)} %bitcast.83), channel_id=1, replica_groups=mesh['col'=16,'row'=2] {'col'}, dimensions={0} | all-to-all | bytes 1048576 | tf_op jit(solution)/shard_map/all_to_all | solution.py:78
  86.0 0.0 copy-start.2
  86.0 0.0 copy-start.3
  86.1 0.0 copy-start.7
  86.1 0.7 copy-done.2
  86.8 0.0 copy-done.3
  86.8 0.0 copy-done.7
  86.8 0.1 fusion.21
  86.9 39.5 %all_gather.14 = bf16[1024,128]{1,0:T(8,128)(2,1)S(1)} all-gather(bf16[64,128]{1,0:T(8,128)(2,1)S(1)} %fusion.21), channel_id=1, replica_groups=mesh['col'=16,'row'=2] {'col'}, dimensions={0}, use_global_device_ids=true | all-gather | bytes 278528 | tf_op jit(solution)/shard_map/all_gather | solution.py:63
  126.4 0.4 convolution_convert_fusion.1
  126.7 0.3 convolution_bitcast_fusion.1
  127.0 0.2 copy.48
  127.2 0.6 fusion.28
  127.8 0.8 copy.49
  128.7 0.0 all-gather.5.cloned.1.call-update
  128.7 5.1 %all-gather.5.cloned.1.call-done = f32[2,1024,128]{2,1,0:T(8,128)} async-done(((f32[1,1024,128]{2,1,0:T(8,128)}), f32[2,1024,128]{2,1,0:T(8,128)}) %all-gather.5.cloned.1.call-update) | async-done | bytes 1048592 | tf_op jit(solution)/shard_map/all_gather | solution.py:68
  133.7 1.3 reduce_sum.42
  135.1 1.3 subtract_convert_fusion
  136.4 0.4 convolution_convert_fusion
  136.7 0.3 convolution_bitcast_fusion
  137.0 0.2 copy.53
  137.3 0.6 fusion.29
  137.9 22.1 %all_to_all.11 = f32[16,64,128]{2,1,0:T(8,128)S(1)} all-to-all(f32[16,64,128]{2,1,0:T(8,128)S(1)} %bitcast.84), channel_id=1, replica_groups=mesh['col'=16,'row'=2] {'col'}, dimensions={0} | all-to-all | bytes 1048576 | tf_op jit(solution)/shard_map/all_to_all | solution.py:78
  160.0 0.7 fusion.14
  (6 shorter events, 0.2 us)
Async XLA Ops:
  7.2 46.3 %copy-start = (bf16[1,1,4,256,256]{4,3,2,1,0:T(8,128)(2,1)S(1)}, bf16[1,1,4,256,256]{4,3,2,1,0:T(8,128)(2,1)}, u32[]{:S(2)}) copy-start(bf16[1,1,4,256,256]{4,3,2,1,0:T(8,128)(2,1)} %param.11) | copy-start | bytes 1572868
  7.2 53.4 %all-gather.3.cloned.1.call-start = ((), (), s32[]{:S(2)}) async-start(), calls=%async_computation.2 | async-start | bytes 1572864 | tf_op jit(solution)/shard_map/all_gather | solution.py:68
  52.5 0.7 copy-start.8
  52.5 0.7 copy-start.9
  55.5 6.4 %copy-start.1 = (f32[1024,128]{1,0:T(8,128)S(1)}, f32[1024,128]{1,0:T(8,128)}, u32[]{:S(2)}) copy-start(f32[1024,128]{1,0:T(8,128)} %param.20) | copy-start | bytes 1572868
  55.5 6.4 %copy-start.4 = (f32[1024]{0:T(1024)S(1)}, f32[1024]{0:T(1024)}, u32[]{:S(2)}) copy-start(f32[1024]{0:T(1024)} %param.16) | copy-start | bytes 12292
  55.5 6.4 %copy-start.5 = (f32[1024]{0:T(1024)S(1)}, f32[1024]{0:T(1024)}, u32[]{:S(2)}) copy-start(f32[1024]{0:T(1024)} %param.15) | copy-start | bytes 12292
  55.5 6.4 %copy-start.6 = (f32[1024]{0:T(1024)S(1)}, f32[1024]{0:T(1024)}, u32[]{:S(2)}) copy-start(f32[1024]{0:T(1024)} %param.17) | copy-start | bytes 12292
  55.5 78.2 %all-gather.5.cloned.1.call-start = ((), (), s32[]{:S(2)}) async-start(), calls=%async_computation.3 | async-start | bytes 1572864 | tf_op jit(solution)/shard_map/all_gather | solution.py:68
  86.0 0.8 copy-start.2
  86.0 0.8 copy-start.3
  86.1 0.7 copy-start.7
Sparse Core Ops, SparseCore 0:
  55.6 4.8 all-gather.2
  128.8 4.8 all-gather.4
